TPU v7x, 128 devices: a whole 4x4x4 slice. The times are simulated.
128 devices in a mesh: base: 8 (over z, core), grp: 16 (over y, x).
Axes of the slice: x: 4, y: 4, z: 4, core: 2. Of those that a mesh axis runs over, the one named last changes fastest.
Arguments:
- q_blocks: bfloat16 [8192, 8, 128, 128], P(('base', 'grp')), may hold values from -0.1875 to 0.1875
- p_blocks: bfloat16 [8192, 16, 128], P(('base', 'grp')), may hold values from -2 to 2
- col_index: int32 [8192, 8], P(('base', 'grp')), may hold values from 0 to 3071, as said below
- agg_of_block: int32 [8192, 1], P(('base', 'grp')), may hold values from 0 to 63; in each aligned block of 64 rows (0 to 63, 64 to 127, ...) at most 2 rows name the same one
Outputs:
- qp_product: float32 [8192, 16, 128], P(('base', 'grp'))
- coarse_rows: float32 [512, 16, 3072], P(('base', 'grp'))
Inputs may be any that keep to these rules, and one draw needn't show every extreme that they name: `col_index`: slot 0 names the row's own block. Slots below 6 have base offset 1 and name a block held by the same grp index or the one just below or above it (cyclically); the other slots have base offset 0 or 2 and name a block held by the same grp index. `agg_of_block`: among the 64 block rows of one device no aggregate occurs more than 2 times, and that count is reached.
All inputs are finite; a program needn't handle non-finite values.
Results may differ from a plain program's by a relative error of at most 0.0003.
Values may be sent and summed in bfloat16 or wider, within the bound.
A program may use at most 128 MiB of HBM per device.

v0:
```python
import jax
import jax.numpy as jnp
from jax import lax
from jax.sharding import PartitionSpec as P


def extended(value, sides, width):
    for axis, dim in sides:
        size, length = (lax.axis_size(axis), value.shape[dim])
        up = [(i, (i + 1) % size) for i in range(size)]
        down = [(j, i) for i, j in up]
        last = lax.slice_in_dim(value, length - width, length, axis=dim)
        first = lax.slice_in_dim(value, 0, width, axis=dim)
        before = lax.ppermute(last, axis, up)
        after = lax.ppermute(first, axis, down)
        value = jnp.concatenate([before, value, after], axis=dim)
    return value


def on_device(q_blocks, p_blocks, col_index, agg_of_block):
    rows = p_blocks.shape[0]
    groups = lax.axis_size("grp")
    group = groups * rows
    grp_pos = lax.axis_index("grp")
    agg_own = agg_of_block[:, 0]
    hp = lax.Precision.HIGHEST
    offset = col_index // group
    target = col_index % group
    local = target % rows
    near_p, near_agg = (
        extended(p_blocks, (("grp", 0),), rows),
        extended(agg_own, (("grp", 0),), rows),
    )
    shard = (target // rows - grp_pos + 1) % groups
    inner_pos = shard * rows + local
    inner_size = 3 * rows
    side_p, side_agg = (
        extended(p_blocks, (("base", 0),), rows),
        extended(agg_own, (("base", 0),), rows),
    )
    table = jnp.concatenate([near_p, side_p[:rows], side_p[2 * rows :]], axis=0)
    agg_table = jnp.concatenate([near_agg, side_agg[:rows], side_agg[2 * rows :]], axis=0)
    position = jnp.where(offset == 1, inner_pos, inner_size + offset // 2 * rows + local)
    picked = table[position]
    colagg = agg_table[position] + offset * rows
    vals = jnp.einsum("inkc,inbc->inkb", picked, q_blocks, preferred_element_type=jnp.float32)
    product = jnp.sum(vals, axis=1)
    wts = jnp.einsum("ikb,inlb->inkl", p_blocks.astype(jnp.float32), vals, precision=hp)
    kdim = wts.shape[2]
    one_col = (colagg[:, :, None] == jnp.arange(3 * rows, dtype=jnp.int32)[None, None, :]).astype(
        jnp.float32
    )
    one_row = (agg_own[:, None] == jnp.arange(rows, dtype=jnp.int32)[None, :]).astype(jnp.float32)
    mixed = jnp.einsum("inc,inkl->ickl", one_col, wts, precision=hp)
    partial_rows = jnp.einsum("ia,ickl->akcl", one_row, mixed, precision=hp).reshape(
        rows, kdim, 3 * rows * kdim
    )
    coarse = lax.psum_scatter(partial_rows, "grp", scatter_dimension=0, tiled=True)
    return (product, coarse)


def solution(mesh):
    placed = (
        P(("base", "grp"), None, None, None),
        P(("base", "grp"), None, None),
        P(("base", "grp"), None),
        P(("base", "grp"), None),
    )
    return jax.shard_map(
        on_device,
        mesh=mesh,
        in_specs=placed,
        out_specs=(P(("base", "grp"), None, None), P(("base", "grp"), None, None)),
        check_vma=False,
    )
```

profile of v0, /device:TPU:33, one launch (start us, length us, event | category | flops | bytes accessed | tf_op | source)
XLA Modules:
  0.0 235.8 jit_solution(11018381453370819006)
XLA Ops:
  7.2 0.0 reduce-scatter.2.cloned.1.call-start
  7.2 0.7 collective-permute-start.7
  7.9 1.6 collective-permute-start.6
  9.4 4.9 %collective-permute-start.5 = (s32[64]{0:T(128)}, s32[64]{0:T(128)S(1)}, u32[]{:S(2)}, u32[]{:S(2)}) collective-permute-start(s32[64]{0:T(128)} %bitcast.30), channel_id=1, source_target_pairs={{1,0},{2,1},{3,2},{4,3},{5,4},{6,5},{7,6},{8,7},{9,8},{10,9},{11,1... | collective-permute-start | bytes 776 | tf_op jit(solution)/shard_map/ppermute | solution.py:15
  14.4 0.8 copy.13
  15.2 0.1 compare_select_fusion
  15.3 0.1 reshape.11
  15.4 0.0 collective-permute-start.3
  15.4 1.7 collective-permute-start.2
  17.1 4.8 %collective-permute-start.1 = (bf16[64,16,128]{2,1,0:T(8,128)(2,1)}, bf16[64,16,128]{2,1,0:T(8,128)(2,1)S(1)}, u32[]{:S(2)}, u32[]{:S(2)}) collective-permute-start(bf16[64,16,128]{2,1,0:T(8,128)(2,1)} %param.5), channel_id=1, source_target_pairs={{1,0},{2,1},{3,2},{4,3},{5,4},{6,5},{7,6},{8,7},{9,8},{10,9},{11,1... | collective-permute-start | bytes 786440 | tf_op jit(solution)/shard_map/ppermute | solution.py:15
  22.0 0.7 concatenate.7
  22.7 3.5 %gather_fusion.1 = s32[512]{0:T(512)S(1)} fusion(s32[320]{0:T(512)S(1)} %concatenate.7, s32[1024]{0:T(1024)S(1)} %pad_clamp_fusion), kind=kCustom, calls=%fused_computation.1 | custom fusion | bytes 6144 | tf_op jit(solution)/shard_map/gather | solution.py:45
  26.2 0.1 reshape.18
  26.4 1.3 collective-permute-done.1
  27.8 2.0 gather_fusion
  29.9 12.3 %fusion.27 = (f32[64,16,128]{2,1,0:T(8,128)}, f32[64,8,16,128]{3,2,1,0:T(8,128)S(1)}) fusion(bf16[64,8,16,128]{3,2,1,0:T(8,128)(2,1)S(1)} %bitcast.27, bf16[64,8,128,128]{3,2,1,0:T(8,128)(2,1)} %param.4), kind=kOutput, calls=%fused_computation.56 | convolution fusion | flops 269352960 | bytes 23592960 | tf_op jit(solution)/shard_map/inkc,inbc->inkb/dot_general | solution.py:46
  42.1 3.4 %convolution_bitcast_fusion = f32[64,8,16,16]{2,3,1,0:T(8,128)} fusion(f32[64,8,16,128]{3,2,1,0:T(8,128)S(1)} %get-tuple-element.5, bf16[64,16,128]{2,1,0:T(8,128)(2,1)S(1)} %copy-done.1), kind=kOutput, calls=%fused_computation.5 | convolution fusion | flops 201326592 | bytes 4980736 | tf_op jit(solution)/shard_map/ikb,inlb->inkl/dot_general | solution.py:48
  45.5 5.6 %copy.17 = f32[64,8,16,16]{3,1,2,0:T(8,128)} copy(f32[64,8,16,16]{2,3,1,0:T(8,128)} %convolution_bitcast_fusion) | data formatting | bytes 1048576 | tf_op jit(solution)/shard_map/ikb,inlb->inkl/transpose | solution.py:48
  51.1 11.5 %fusion.6 = f32[64,192,16,16]{1,3,2,0:T(8,128)} fusion(f32[64,8,16,16]{3,1,2,0:T(8,128)} %copy.17, s32[64,8]{1,0:T(8,128)S(1)} %multiply_add_fusion), kind=kOutput, calls=%fused_computation.8 | convolution fusion | flops 302088192 | bytes 13109248 | tf_op jit(solution)/shard_map/inc,inkl->ickl/dot_general | solution.py:54
  62.6 26.9 %fusion.2 = f32[64,16,192,16]{2,0,3,1:T(8,128)} fusion(f32[64,192,16,16]{1,3,2,0:T(8,128)} %fusion.6, s32[64]{0:T(128)S(1)} %bitcast.33), kind=kOutput, calls=%fused_computation.4 | convolution fusion | flops 2415923200 | bytes 25166080 | tf_op jit(solution)/shard_map/ia,ickl->akcl/dot_general | solution.py:55
  89.6 23.1 %copy.19 = f32[64,16,192,16]{0,3,2,1:T(8,128)} copy(f32[64,16,192,16]{2,0,3,1:T(8,128)} %fusion.2) | data formatting | bytes 25165824 | tf_op jit(solution)/shard_map/ia,ickl->akcl/transpose | solution.py:55
  112.6 20.0 %copy.20 = f32[64,16,3072]{2,1,0:T(8,128)} copy(f32[64,16,3072]{0,2,1:T(8,128)} %bitcast.26) | data formatting | bytes 25165824 | tf_op jit(solution)/shard_map/reshape | solution.py:55
  132.6 0.0 reduce-scatter.2.cloned.1.call-update
  132.6 96.4 %reduce-scatter.2.cloned.1.call-done = f32[4,16,3072]{2,1,0:T(8,128)} async-done(((f32[64,16,3072]{2,1,0:T(8,128)}), f32[4,16,3072]{2,1,0:T(8,128)}) %reduce-scatter.2.cloned.1.call-update) | async-done | bytes 786448 | tf_op jit(solution)/shard_map/reduce_scatter | solution.py:58
  (22 shorter events, 0.2 us)
Async XLA Ops:
  7.2 221.8 %reduce-scatter.2.cloned.1.call-start = ((), (), s32[]{:S(2)}) async-start(), calls=%async_computation.1 | async-start | bytes 13369344 | tf_op jit(solution)/shard_map/reduce_scatter | solution.py:58
  7.2 8.2 %collective-permute-start.7 = (s32[64]{0:T(128)}, s32[64]{0:T(128)S(1)}, u32[]{:S(2)}, u32[]{:S(2)}) collective-permute-start(s32[64]{0:T(128)} %bitcast.28), channel_id=1, source_target_pairs={{16,0},{32,16},{48,32},{64,48},{80,64},{96,80},{112,96},{0,112},{1... | collective-permute-start | bytes 776 | tf_op jit(solution)/shard_map/ppermute | solution.py:15
  7.9 7.5 %collective-permute-start.6 = (s32[64]{0:T(128)}, s32[64]{0:T(128)S(1)}, u32[]{:S(2)}, u32[]{:S(2)}) collective-permute-start(s32[64]{0:T(128)} %bitcast.29), channel_id=1, source_target_pairs={{0,16},{16,32},{32,48},{48,64},{64,80},{80,96},{96,112},{112,0},{1... | collective-permute-start | bytes 776 | tf_op jit(solution)/shard_map/ppermute | solution.py:14
  9.4 7.7 %collective-permute-start.5 = (s32[64]{0:T(128)}, s32[64]{0:T(128)S(1)}, u32[]{:S(2)}, u32[]{:S(2)}) collective-permute-start(s32[64]{0:T(128)} %bitcast.30), channel_id=1, source_target_pairs={{1,0},{2,1},{3,2},{4,3},{5,4},{6,5},{7,6},{8,7},{9,8},{10,9},{11,1... | collective-permute-start | bytes 776 | tf_op jit(solution)/shard_map/ppermute | solution.py:15
  14.4 7.6 %collective-permute-start.4 = (s32[64]{0:T(128)}, s32[64]{0:T(128)S(1)}, u32[]{:S(2)}, u32[]{:S(2)}) collective-permute-start(s32[64]{0:T(128)} %bitcast.31), channel_id=1, source_target_pairs={{0,1},{1,2},{2,3},{3,4},{4,5},{5,6},{6,7},{7,8},{8,9},{9,10},{10,1... | collective-permute-start | bytes 776 | tf_op jit(solution)/shard_map/ppermute | solution.py:14
  14.4 11.9 %collective-permute-start = (bf16[64,16,128]{2,1,0:T(8,128)(2,1)}, bf16[64,16,128]{2,1,0:T(8,128)(2,1)S(1)}, u32[]{:S(2)}, u32[]{:S(2)}) collective-permute-start(bf16[64,16,128]{2,1,0:T(8,128)(2,1)} %param.5), channel_id=1, source_target_pairs={{0,1},{1,2},{2,3},{3,4},{4,5},{5,6},{6,7},{7,8},{8,9},{9,10},{10,1... | collective-permute-start | bytes 786440 | tf_op jit(solution)/shard_map/ppermute | solution.py:14
  15.4 12.4 %collective-permute-start.3 = (bf16[64,16,128]{2,1,0:T(8,128)(2,1)}, bf16[64,16,128]{2,1,0:T(8,128)(2,1)S(1)}, u32[]{:S(2)}, u32[]{:S(2)}) collective-permute-start(bf16[64,16,128]{2,1,0:T(8,128)(2,1)} %param.5), channel_id=1, source_target_pairs={{16,0},{32,16},{48,32},{64,48},{80,64},{96,80},{112,96},{0,112},{1... | collective-permute-start | bytes 786440 | tf_op jit(solution)/shard_map/ppermute | solution.py:15
  15.4 12.3 %collective-permute-start.2 = (bf16[64,16,128]{2,1,0:T(8,128)(2,1)}, bf16[64,16,128]{2,1,0:T(8,128)(2,1)S(1)}, u32[]{:S(2)}, u32[]{:S(2)}) collective-permute-start(bf16[64,16,128]{2,1,0:T(8,128)(2,1)} %param.5), channel_id=1, source_target_pairs={{0,16},{16,32},{32,48},{48,64},{64,80},{80,96},{96,112},{112,0},{1... | collective-permute-start | bytes 786440 | tf_op jit(solution)/shard_map/ppermute | solution.py:14
  17.1 10.5 %collective-permute-start.1 = (bf16[64,16,128]{2,1,0:T(8,128)(2,1)}, bf16[64,16,128]{2,1,0:T(8,128)(2,1)S(1)}, u32[]{:S(2)}, u32[]{:S(2)}) collective-permute-start(bf16[64,16,128]{2,1,0:T(8,128)(2,1)} %param.5), channel_id=1, source_target_pairs={{1,0},{2,1},{3,2},{4,3},{5,4},{6,5},{7,6},{8,7},{9,8},{10,9},{11,1... | collective-permute-start | bytes 786440 | tf_op jit(solution)/shard_map/ppermute | solution.py:15
  22.7 3.7 %copy-start = (bf16[64,16,128]{2,1,0:T(8,128)(2,1)S(1)}, bf16[64,16,128]{2,1,0:T(8,128)(2,1)}, u32[]{:S(2)}) copy-start(bf16[64,16,128]{2,1,0:T(8,128)(2,1)} %param.5) | copy-start | bytes 786436
  29.8 12.3 %copy-start.1 = (bf16[64,16,128]{2,1,0:T(8,128)(2,1)S(1)}, bf16[64,16,128]{2,1,0:T(8,128)(2,1)}, u32[]{:S(2)}) copy-start(bf16[64,16,128]{2,1,0:T(8,128)(2,1)} %param.5) | copy-start | bytes 786436
  51.1 11.5 %copy-start.2 = (s32[64,1]{0,1:T(1,128)S(1)}, s32[64,1]{0,1:T(1,128)}, u32[]{:S(2)}) copy-start(s32[64,1]{0,1:T(1,128)} %param.7) | copy-start | bytes 772
Sparse Core Ops, SparseCore 0:
  132.7 96.2 reduce-scatter.1
where the time goes:
time: 238 us; the launch traced here: 236 us
  waiting for transfers between devices  97.7 us (41%)
  local copies, waits for them, and re-layouts  56 us (24%)
  matrix products  54.1 us (23%)
  between operations  14.2 us (6%)
  starting transfers between devices  13.8 us (6%)
    reduce_scatter x1, waiting for transfers between devices, on_device(): lax.psum_scatter(partial_rows, 'grp', scatter_dimension=0, tiled=True)  96.4 us
    dot_general x1, matrix products, on_device(): jnp.einsum('ia,ickl->akcl', one_row, mixed, precision=hp)  26.9 us
    transpose x1, local copies, waits for them, and re-layouts, on_device(): jnp.einsum('ia,ickl->akcl', one_row, mixed, precision=hp)  23.1 us
    reshape x1, local copies, waits for them, and re-layouts, on_device(): jnp.einsum('ia,ickl->akcl', one_row, mixed, precision=hp)  20 us
    dot_general x1, matrix products, on_device(): jnp.einsum('inkc,inbc->inkb', picked, q_blocks, preferred_element_type=jn...  12.3 us
    dot_general x1, matrix products, on_device(): mixed = jnp.einsum('inc,inkl->ickl', one_col, wts, precision=hp)  11.5 us
    ppermute x4, starting transfers between devices, extended(): after = lax.ppermute(first, axis, down)  10.5 us
    transpose x1, local copies, waits for them, and re-layouts, on_device(): jnp.einsum('ikb,inlb->inkl', p_blocks.astype(jnp.float32), vals, precisio...  5.61 us
  transfers between devices with their start and end apart: 9, of which 2 were waited for; matrix products, arithmetic and copies ran while one was open for 2% of the time, Pallas kernels for 0%

commit v1 on v0

v1 whole, which is shorter than its diff:
```python
import functools

import jax
import jax.numpy as jnp
from jax import lax
from jax.experimental import pallas as pl
from jax.experimental.pallas import tpu as pltpu
from jax.sharding import PartitionSpec as P

F32, BF16, I32 = jnp.float32, jnp.bfloat16, jnp.int32
MESH = pl.DeviceIdType.MESH
R, NB, NB_IN, K, B = 64, 8, 6, 16, 128
N_BASE, N_GRP = 8, 16
OWN = 4
SLOTS = 2 * OWN
CH = 24
PAIRS = ((6, 7), (0, 1), (2, 3), (4, 5))


def dot_t(a, b):
    return lax.dot_general(a, b, (((1,), (1,)), ((), ())), preferred_element_type=F32)


def iota(shape, dim):
    return lax.broadcasted_iota(I32, shape, dim)


def product_kernel(
    col_s, col_v, agg_v, q_hbm, p_hbm,
    prod, w_in, meta_in,
    q_v, near, side, aggtab, pos, split, w_v, pack, meta, order_v, order_s,
    q_sem, own_sem, p_send, p_recv, a_send, a_recv, w_send, w_recv, m_send, m_recv, loc_sem,
):
    base, grp = lax.axis_index("base"), lax.axis_index("grp")
    sends = (
        ({"grp": (grp + 1) % N_GRP}, near, 0, 0),
        ({"grp": (grp + N_GRP - 1) % N_GRP}, near, 2, 2),
        ({"base": (base + 1) % N_BASE}, side, 0, 3),
        ({"base": (base + N_BASE - 1) % N_BASE}, side, 1, 4),
    )
    q_copies = [
        pltpu.make_async_copy(q_hbm.at[:, pl.ds(a, 2)], q_v.at[:, pl.ds(a, 2)], q_sem.at[c])
        for c, (a, _) in enumerate(PAIRS)
    ]
    own_copy = pltpu.make_async_copy(p_hbm, near.at[pl.ds(R, R)], own_sem)
    own_copy.start()
    barrier = pltpu.get_barrier_semaphore()
    for d in range(1, N_GRP):
        pl.semaphore_signal(barrier, 1, device_id={"grp": (grp + d) % N_GRP}, device_id_type=MESH)
    for d in (1, N_BASE - 1):
        pl.semaphore_signal(barrier, 1, device_id={"base": (base + d) % N_BASE}, device_id_type=MESH)
    for c in q_copies:
        c.start()

    row, lane = iota((R, B), 0), iota((R, B), 1)
    agg_col = agg_v[...].astype(F32)
    agg_row = jnp.sum(jnp.where(row == lane, agg_col, 0.0), axis=0, keepdims=True)
    aggtab[1] = jnp.broadcast_to(agg_row, (8, B))

    pl.semaphore_wait(barrier, N_GRP + 1)
    p_copies, a_copies = [], []
    for s, (to, tab, part, seg) in enumerate(sends):
        p_copies.append(
            pltpu.make_async_remote_copy(
                p_hbm, tab.at[pl.ds(part * R, R)], p_send.at[s], p_recv.at[s], device_id=to, device_id_type=MESH
            )
        )
        a_copies.append(
            pltpu.make_async_remote_copy(
                aggtab.at[1], aggtab.at[seg], a_send.at[s], a_recv.at[s], device_id=to, device_id_type=MESH
            )
        )
    for c in p_copies + a_copies:
        c.start()

    before = (agg_col == agg_row) & (lane < row)
    rank = jnp.sum(jnp.where(before, 1.0, 0.0), axis=1, keepdims=True)
    match = (2.0 * agg_col + rank) == lane.astype(F32)
    order = jnp.sum(jnp.where(match, row.astype(F32), 0.0), axis=0, keepdims=True)
    order_v[...] = jnp.broadcast_to(order, (8, B)).astype(I32)
    order_copy = pltpu.make_async_copy(order_v, order_s, loc_sem.at[0])
    order_copy.start()

    def position(c, slot):
        if slot >= NB_IN:
            return (c >> 11) * R + (c & (R - 1))
        shard = jnp.minimum(((c >> 6) - grp + 1) & (N_GRP - 1), 2)
        return shard * R + (c & (R - 1))

    @pl.loop(0, R)
    def _(i):
        for n in range(NB):
            pos[i, n] = position(col_s[i, n], n)

    def values(pair, i):
        a, b = pair
        tab = side if a >= NB_IN else near
        zero = jnp.zeros((K, B), BF16)
        left, right = [], []
        for d in range(2):
            left += [tab[pos[i + d, a]], zero]
            right += [zero, tab[pos[i + d, b]]]
        lhs = jnp.concatenate([jnp.concatenate(left, 0), jnp.concatenate(right, 0)], 1)
        rhs = jnp.concatenate([jnp.concatenate([q_v[i + d, a], q_v[i + d, b]], 1) for d in range(2)], 0)
        out = dot_t(lhs, rhs)
        sums = []
        for d in range(2):
            v = out[2 * d * K : 2 * (d + 1) * K, d * B : (d + 1) * B]
            high = v.astype(BF16)
            split[i + d, a * K : (a + 2) * K, :B] = high
            split[i + d, a * K : (a + 2) * K, B:] = (v - high.astype(F32)).astype(BF16)
            sums.append(v[:K] + v[K:])
        return sums

    own_copy.wait()
    for s in (2, 3):
        p_copies[s].wait_recv()
    q_copies[0].wait()

    @pl.loop(0, R // 16)
    def _(j):
        for u in range(0, 16, 2):
            i = j * 16 + u
            for d, v in enumerate(values(PAIRS[0], i)):
                prod[i + d] = v

    for c in a_copies:
        c.wait_recv()
    col = col_v[...]
    colagg = jnp.where(lane == NB, 1.0, 0.0)
    for n in range(NB):
        at = position(col[:, n : n + 1], n)
        found = jnp.zeros((R, B), F32)
        for part, seg in enumerate((3, 4) if n >= NB_IN else (0, 1, 2)):
            found = found + jnp.where(at - part * R == lane, aggtab[seg, 0:1], 0.0)
        total = jnp.sum(found, axis=1, keepdims=True) + ((col[:, n : n + 1] >> 10) * R).astype(F32)
        colagg = jnp.where(lane == n, total, colagg)
    placed = lax.dot_general(
        jnp.where(match, 1.0, 0.0).astype(BF16), colagg.astype(BF16), (((0,), (0,)), ((), ())),
        preferred_element_type=F32,
    )
    meta[...] = placed.astype(I32).reshape(N_GRP, SLOTS, B)

    for s in (0, 1):
        p_copies[s].wait_recv()
    for c in q_copies[1:]:
        c.wait()

    @pl.loop(0, R // 16)
    def _(j):
        for u in range(0, 16, 2):
            i = j * 16 + u
            all_sums = [values(pair, i) for pair in PAIRS[1:]]
            for d in range(2):
                prod[i + d] += all_sums[0][d] + all_sums[1][d] + all_sums[2][d]

    @pl.loop(0, R // 16)
    def _(j):
        for u in range(0, 16, 2):
            i = j * 16 + u
            p_two = near[pl.ds(R + i, 2)].reshape(2 * K, B)
            out = dot_t(jnp.concatenate([p_two, p_two], 1), split[pl.ds(i, 2)].reshape(2 * B, 2 * B))
            w_v[i] = out[:K, :B]
            w_v[i + 1] = out[K:, B:]

    order_copy.wait()

    def gathered(d, to):
        for t in range(SLOTS):
            pack[d, t] = w_v[order_s[0, to * SLOTS + t] & (R - 1)]

    copies = []
    for d in range(1, N_GRP):
        to = (grp + d) % N_GRP
        gathered(d, to)
        for src, dst, send, recv in (
            (pack.at[d], w_in.at[grp], w_send, w_recv),
            (meta.at[to], meta_in.at[grp], m_send, m_recv),
        ):
            copies.append(
                pltpu.make_async_remote_copy(
                    src, dst, send.at[d], recv.at[d], device_id={"grp": to}, device_id_type=MESH
                )
            )
            copies[-1].start()
    gathered(0, grp)
    w_own = pltpu.make_async_copy(pack.at[0], w_in.at[grp], loc_sem.at[1])
    m_own = pltpu.make_async_copy(meta.at[grp], meta_in.at[grp], loc_sem.at[2])
    w_own.start()
    m_own.start()
    for c in p_copies + a_copies:
        c.wait_send()
    w_own.wait()
    m_own.wait()
    for c in copies:
        c.wait()


def coarse_kernel(meta, w, prod_in, coarse, prod_out, acc0, acc1, acc2, acc3, sem):
    copy = pltpu.make_async_copy(prod_in, prod_out, sem)
    copy.start()
    accs = (acc0, acc1, acc2, acc3)
    for acc in accs:
        acc[...] = jnp.zeros_like(acc)
    group = iota((K, B), 1) >> 4

    @pl.loop(0, N_GRP)
    def _(src):
        for t in range(2):
            for n in range(NB):
                for a, acc in enumerate(accs):
                    s = 2 * a + t
                    c = meta[src, s, n]
                    low = c & 7
                    turned = pltpu.roll(w[src, s], ((low - n) & 7) * K, 1)
                    here = jnp.where(meta[src, s, NB] == 1, low, -1)
                    acc[c >> 3] += jnp.where(group == here, turned, 0.0)

    for a, acc in enumerate(accs):
        for h in range(CH):
            coarse[a, :, h * B : (h + 1) * B] = acc[h]
    copy.wait()


def on_device(q_blocks, p_blocks, col_index, agg_of_block):
    vmem, smem = pl.BlockSpec(memory_space=pltpu.VMEM), pl.BlockSpec(memory_space=pltpu.SMEM)
    any_ = pl.BlockSpec(memory_space=pl.ANY)
    dma = pltpu.SemaphoreType.DMA
    prod, w_in, meta_in = pl.pallas_call(
        product_kernel,
        in_specs=[smem, vmem, vmem, any_, any_],
        out_specs=[vmem, any_, any_],
        out_shape=[
            jax.ShapeDtypeStruct((R, K, B), F32),
            jax.ShapeDtypeStruct((N_GRP, SLOTS, K, B), F32),
            jax.ShapeDtypeStruct((N_GRP, SLOTS, B), I32),
        ],
        scratch_shapes=[
            pltpu.VMEM((R, NB, B, B), BF16),
            pltpu.VMEM((3 * R, K, B), BF16),
            pltpu.VMEM((2 * R, K, B), BF16),
            pltpu.VMEM((5, 8, B), F32),
            pltpu.SMEM((R, NB), I32),
            pltpu.VMEM((R, B, 2 * B), BF16),
            pltpu.VMEM((R, K, B), F32),
            pltpu.VMEM((N_GRP, SLOTS, K, B), F32),
            pltpu.VMEM((N_GRP, SLOTS, B), I32),
            pltpu.VMEM((8, B), I32),
            pltpu.SMEM((8, B), I32),
            dma((4,)),
            dma,
            dma((4,)),
            dma((4,)),
            dma((4,)),
            dma((4,)),
            dma((N_GRP,)),
            dma((N_GRP,)),
            dma((N_GRP,)),
            dma((N_GRP,)),
            dma((3,)),
        ],
        compiler_params=pltpu.CompilerParams(
            collective_id=0, has_side_effects=True, vmem_limit_bytes=40 << 20
        ),
        name="products",
    )(col_index, col_index, agg_of_block, q_blocks, p_blocks)
    coarse, product = pl.pallas_call(
        coarse_kernel,
        in_specs=[smem, vmem, any_],
        out_specs=[vmem, any_],
        out_shape=[
            jax.ShapeDtypeStruct((OWN, K, CH * B), F32),
            jax.ShapeDtypeStruct((R, K, B), F32),
        ],
        scratch_shapes=[pltpu.VMEM((CH, K, B), F32)] * OWN + [dma],
        compiler_params=pltpu.CompilerParams(vmem_limit_bytes=16 << 20),
        name="coarse",
    )(meta_in, w_in, prod)
    return product, coarse


def solution(mesh):
    placed = (
        P(("base", "grp"), None, None, None),
        P(("base", "grp"), None, None),
        P(("base", "grp"), None),
        P(("base", "grp"), None),
    )
    return jax.shard_map(
        on_device,
        mesh=mesh,
        in_specs=placed,
        out_specs=(P(("base", "grp"), None, None), P(("base", "grp"), None, None)),
        check_vma=False,
    )
```

time: 238 us -> 50.9 us (0.21)
  waiting for transfers between devices: 97.7 us -> 0 us
  matrix products: 54.1 us -> 0 us
  local copies, waits for them, and re-layouts: 56 us -> 2.46 us
  Pallas kernels: 0 us -> 47.6 us
  starting transfers between devices: 13.8 us -> 0 us
  between operations: 14.2 us -> 0.64 us
    reduce_scatter x1 -> x0, waiting for transfers between devices: 96.4 us -> none  [on_device(): lax.psum_scatter(partial_rows, 'grp', scatter_dimension=0, tiled=True)]
    dot_general x4 -> x0, matrix products: 54.1 us -> none  [the longest x1 26.9 us: on_device(): jnp.einsum('ia,ickl->akcl', one_row, mixed, precision=hp)]
    pallas_call x0 -> x2, Pallas kernels: none -> 47.6 us  [the longest x1 40.2 us: on_device(): pl.pallas_call(product_kernel, in_specs=[smem, vmem, vmem, any_, any_], o...]
    transpose x2 -> x0, local copies, waits for them, and re-layouts: 28.7 us -> none  [the longest x1 23.1 us: on_device(): jnp.einsum('ia,ickl->akcl', one_row, mixed, precision=hp)]
    reshape x1 -> x0, local copies, waits for them, and re-layouts: 20 us -> none  [on_device(): jnp.einsum('ia,ickl->akcl', one_row, mixed, precision=hp)]
    ppermute x8 -> x0, starting transfers between devices: 13.7 us -> none  [the longest x4 10.5 us: extended(): after = lax.ppermute(first, axis, down)]
    gather x3 -> x0, local copies, waits for them, and re-layouts: 5.59 us -> none  [the longest x2 3.57 us: on_device(): colagg = agg_table[position] + offset * rows]
  transfers between devices with their start and end apart: 9 -> 0, of which waited for: 2 -> 0; matrix products, arithmetic and copies ran while one was open for 2% -> 0% of each run, Pallas kernels for 0% -> 0%
where the time goes in v1:
time: 50.9 us; the launch traced here: 50.7 us
  Pallas kernels  47.6 us (94%)
  local copies, waits for them, and re-layouts  2.46 us (5%)
  between operations  0.64 us (1%)
    pallas_call x1, Pallas kernels, on_device(): pl.pallas_call(product_kernel, in_specs=[smem, vmem, vmem, any_, any_], o...  40.2 us
    pallas_call x1, Pallas kernels, on_device(): pl.pallas_call(coarse_kernel, in_specs=[smem, vmem, any_], out_specs=[vme...  7.41 us
    unnamed x4, local copies, waits for them, and re-layouts  2.46 us

profile of v1, /device:TPU:33, one launch (start us, length us, event | category | flops | bytes accessed | tf_op | source)
XLA Modules:
  0.0 50.7 jit_solution(4930268379007308990)
XLA Ops:
  0.6 0.8 %copy.6.col_s.col_v = s32[64,8]{1,0:T(8,128)S(1)} copy(s32[64,8]{0,1:T(8,128)} %param.6) | data formatting | bytes 4096 | tf_op args[2]
  1.4 0.7 %copy.8.agg_v = s32[64,1]{1,0:T(8,128)S(1)} copy(s32[64,1]{0,1:T(1,128)} %param.7) | data formatting | bytes 512 | tf_op args[3]
  2.1 0.0 copy-start
  2.1 0.9 %copy-done = bf16[64,16,128]{2,1,0:T(8,128)(2,1)S(1)} copy-done((bf16[64,16,128]{2,1,0:T(8,128)(2,1)S(1)}, bf16[64,16,128]{2,1,0:T(8,128)(2,1)}, u32[]{:S(2)}) %copy-start) | copy-done | bytes 262168
  3.1 40.2 %products.1 = (f32[64,16,128]{2,1,0:T(8,128)S(1)}, f32[16,8,16,128]{3,2,1,0:T(8,128)S(1)}, s32[16,8,128]{2,1,0:T(8,128)S(1)}) custom-call(s32[64,8]{1,0:T(8,128)S(1)} %copy.6.col_s.col_v, s32[64,8]{1,0:T(8,128)S(1)} %copy.6.col_s.col_v, s32[64,1]{1,0:T(8,128)S(1)} %copy.8.agg_v, bf16[64,8,128,128]{3,2,1,0:T(8,128)(2,1)} %q_hbm.1, ...), custom_call_target="tpu_custom_call" | custom-call | tf_op jit(solution)/shard_map/products/pallas_call | solution.py:229
  43.3 7.4 %coarse.1 = (f32[4,16,3072]{2,1,0:T(8,128)}, f32[64,16,128]{2,1,0:T(8,128)}) custom-call(s32[16,8,128]{2,1,0:T(8,128)S(1)} %get-tuple-element.7.meta, f32[16,8,16,128]{3,2,1,0:T(8,128)S(1)} %get-tuple-element.8.w, f32[64,16,128]{2,1,0:T(8,128)S(1)} %get-tuple-element.9.prod_in), custom_call_target="tpu_custom_call" | custom-call | tf_op jit(solution)/shard_map/coarse/pallas_call | solution.py:267
Async XLA Ops:
  2.1 0.9 %copy-start = (bf16[64,16,128]{2,1,0:T(8,128)(2,1)S(1)}, bf16[64,16,128]{2,1,0:T(8,128)(2,1)}, u32[]{:S(2)}) copy-start(bf16[64,16,128]{2,1,0:T(8,128)(2,1)} %p_hbm.1) | copy-start | bytes 786436

commit v2 on v1

v2 whole, which is shorter than its diff:
```python
import functools

import jax
import jax.numpy as jnp
from jax import lax
from jax.experimental import pallas as pl
from jax.experimental.pallas import tpu as pltpu
from jax.sharding import PartitionSpec as P

F32, BF16, I32 = jnp.float32, jnp.bfloat16, jnp.int32
MESH = pl.DeviceIdType.MESH
R, NB, NB_IN, K, B = 64, 8, 6, 16, 128
N_BASE, N_GRP = 8, 16
OWN = 4
SLOTS = 2 * OWN
STEPS = 32000.0
CH = 24
PAIRS = ((6, 7), (0, 1), (2, 3), (4, 5))


def dot_t(a, b):
    return lax.dot_general(a, b, (((1,), (1,)), ((), ())), preferred_element_type=F32)


def iota(shape, dim):
    return lax.broadcasted_iota(I32, shape, dim)


def product_kernel(
    col_hbm, agg_hbm, q_hbm, p_hbm,
    prod, w_in, meta_in,
    q_v, near, side, col_s, col_v, agg_v, aggtab, split, w_v, pack, info, meta, order_v, order_s,
    q_sem, loc_sem, p_send, p_recv, a_send, a_recv, w_send, w_recv, m_send, m_recv,
):
    base, grp = lax.axis_index("base"), lax.axis_index("grp")
    barrier = pltpu.get_barrier_semaphore()
    for d in range(1, N_GRP):
        pl.semaphore_signal(barrier, 1, device_id={"grp": (grp + d) % N_GRP}, device_id_type=MESH)
    for d in (1, N_BASE - 1):
        pl.semaphore_signal(barrier, 1, device_id={"base": (base + d) % N_BASE}, device_id_type=MESH)
    sends = (
        ({"grp": (grp + 1) % N_GRP}, near, 0, 0),
        ({"grp": (grp + N_GRP - 1) % N_GRP}, near, 2, 2),
        ({"base": (base + 1) % N_BASE}, side, 0, 3),
        ({"base": (base + N_BASE - 1) % N_BASE}, side, 1, 4),
    )
    agg_copy = pltpu.make_async_copy(agg_hbm, agg_v, loc_sem.at[0])
    col_copies = (
        pltpu.make_async_copy(col_hbm, col_s, loc_sem.at[1]),
        pltpu.make_async_copy(col_hbm, col_v, loc_sem.at[2]),
    )
    own_copy = pltpu.make_async_copy(p_hbm, near.at[pl.ds(R, R)], loc_sem.at[3])
    for c in (agg_copy, *col_copies, own_copy):
        c.start()
    q_copies = [
        pltpu.make_async_copy(q_hbm.at[:, pl.ds(a, 2)], q_v.at[:, pl.ds(a, 2)], q_sem.at[c])
        for c, (a, _) in enumerate(PAIRS)
    ]
    for c in q_copies:
        c.start()

    row, lane = iota((R, B), 0), iota((R, B), 1)
    agg_copy.wait()
    agg_row = jnp.concatenate([agg_v[...], jnp.zeros((1, B - R), I32)], 1).astype(F32)
    aggtab[1] = jnp.broadcast_to(agg_row, (8, B))

    pl.semaphore_wait(barrier, N_GRP + 1)
    p_copies, a_copies = [], []
    for s, (to, tab, part, seg) in enumerate(sends):
        p_copies.append(
            pltpu.make_async_remote_copy(
                p_hbm, tab.at[pl.ds(part * R, R)], p_send.at[s], p_recv.at[s], device_id=to, device_id_type=MESH
            )
        )
        a_copies.append(
            pltpu.make_async_remote_copy(
                aggtab.at[1], aggtab.at[seg], a_send.at[s], a_recv.at[s], device_id=to, device_id_type=MESH
            )
        )
    for c in a_copies + p_copies:
        c.start()

    agg_col = jnp.sum(jnp.where(row == lane, agg_row, 0.0), axis=1, keepdims=True)
    before = (agg_col == agg_row) & (lane < row)
    rank = jnp.sum(jnp.where(before, 1.0, 0.0), axis=1, keepdims=True)
    match = (2.0 * agg_col + rank) == lane.astype(F32)
    order = jnp.sum(jnp.where(match, row.astype(F32), 0.0), axis=0, keepdims=True)
    order_v[...] = jnp.broadcast_to(order, (8, B)).astype(I32)
    order_copy = pltpu.make_async_copy(order_v, order_s, loc_sem.at[4])
    order_copy.start()

    def position(c, slot):
        if slot >= NB_IN:
            return (c >> 11) * R + (c & (R - 1))
        shard = jnp.minimum(((c >> 6) - grp + 1) & (N_GRP - 1), 2)
        return shard * R + (c & (R - 1))

    def values(pair, i):
        a, b = pair
        tab = side if a >= NB_IN else near
        zero = jnp.zeros((K, B), BF16)
        left, right = [], []
        for d in range(2):
            left += [tab[position(col_s[a, i + d], a)], zero]
            right += [zero, tab[position(col_s[b, i + d], b)]]
        lhs = jnp.concatenate([jnp.concatenate(left, 0), jnp.concatenate(right, 0)], 1)
        rhs = jnp.concatenate([jnp.concatenate([q_v[i + d, a], q_v[i + d, b]], 1) for d in range(2)], 0)
        out = dot_t(lhs, rhs)
        sums = []
        for d in range(2):
            v = out[2 * d * K : 2 * (d + 1) * K, d * B : (d + 1) * B]
            high = v.astype(BF16)
            split[i + d, a * K : (a + 2) * K, :B] = high
            split[i + d, a * K : (a + 2) * K, B:] = (v - high.astype(F32)).astype(BF16)
            sums.append(v[:K] + v[K:])
        return sums

    for c in col_copies:
        c.wait()
    for c in a_copies:
        c.wait_recv()
    col = jnp.concatenate([col_v[...], jnp.zeros((NB, B - R), I32)], 1)
    near_at, side_at = position(col, 0), position(col, NB_IN)

    def looked_up(low, high, at):
        table = jnp.concatenate([aggtab[low][:, :R], aggtab[high][:, :R]], 1)
        return jnp.take_along_axis(table, at, axis=1)

    inner = jnp.where(near_at < B, looked_up(0, 1, near_at & (B - 1)), looked_up(2, 2, near_at & (B - 1)))
    outer = looked_up(3, 4, side_at & (B - 1))
    colagg = jnp.where(iota((NB, B), 0) < NB_IN, inner, outer) + ((col >> 10) * R).astype(F32)
    info[...] = jnp.zeros_like(info)
    info[:NB] = colagg
    info[NB : NB + 1] = jnp.ones((1, B), F32)

    own_copy.wait()
    for s in (2, 3):
        p_copies[s].wait_recv()
    q_copies[0].wait()

    @pl.loop(0, R // 16)
    def _(j):
        for u in range(0, 16, 2):
            i = j * 16 + u
            for d, v in enumerate(values(PAIRS[0], i)):
                prod[i + d] = v

    for s in (0, 1):
        p_copies[s].wait_recv()
    for c in q_copies[1:]:
        c.wait()

    @pl.loop(0, R // 16)
    def _(j):
        for u in range(0, 16, 2):
            i = j * 16 + u
            all_sums = [values(pair, i) for pair in PAIRS[1:]]
            for d in range(2):
                prod[i + d] += all_sums[0][d] + all_sums[1][d] + all_sums[2][d]

    spot = iota((K, B), 1)

    @pl.loop(0, R // 16)
    def _(j):
        widths = info[K : 2 * K]
        for u in range(0, 16, 2):
            i = j * 16 + u
            p_two = near[pl.ds(R + i, 2)].reshape(2 * K, B)
            out = dot_t(jnp.concatenate([p_two, p_two], 1), split[pl.ds(i, 2)].reshape(2 * B, 2 * B))
            for d in range(2):
                w = out[d * K : (d + 1) * K, d * B : (d + 1) * B]
                most = jnp.max(jnp.abs(w), axis=1, keepdims=True)
                width = jnp.maximum(1.01 * most, 1e-30).astype(BF16).astype(F32)
                w_v[i + d] = jnp.round(w * (STEPS / width)).astype(I32).astype(jnp.int16)
                widths = jnp.where(spot == i + d, width, widths)
        info[K : 2 * K] = widths

    meta[...] = lax.dot_general(
        jnp.where(match, 1.0, 0.0).astype(BF16), info[:, :R].astype(BF16), (((0,), (1,)), ((), ())),
        preferred_element_type=F32,
    ).reshape(N_GRP, SLOTS, B)
    order_copy.wait()

    def gathered(d, to):
        for t in range(SLOTS):
            pack[d, t] = w_v[order_s[0, to * SLOTS + t] & (R - 1)]

    copies = []
    for d in range(1, N_GRP):
        to = (grp + d) % N_GRP
        gathered(d, to)
        for src, dst, send, recv in (
            (pack.at[d], w_in.at[grp], w_send, w_recv),
            (meta.at[to], meta_in.at[grp], m_send, m_recv),
        ):
            copies.append(
                pltpu.make_async_remote_copy(
                    src, dst, send.at[d], recv.at[d], device_id={"grp": to}, device_id_type=MESH
                )
            )
            copies[-1].start()
    gathered(0, grp)
    w_own = pltpu.make_async_copy(pack.at[0], w_in.at[grp], loc_sem.at[5])
    m_own = pltpu.make_async_copy(meta.at[grp], meta_in.at[grp], loc_sem.at[6])
    w_own.start()
    m_own.start()
    for c in p_copies + a_copies:
        c.wait_send()
    w_own.wait()
    m_own.wait()
    for c in copies:
        c.wait()


def coarse_kernel(
    meta, w, prod_in, coarse, prod_out, acc0, acc1, acc2, acc3, place_v, place_s, listed, count, sem
):
    copy = pltpu.make_async_copy(prod_in, prod_out, sem.at[0])
    copy.start()
    accs = (acc0, acc1, acc2, acc3)
    turned = meta[...].T
    widths = turned[K : 2 * K] * (1.0 / STEPS)
    slot = iota((K, B), 0)
    col = turned[:K].astype(I32)
    low = col & 7
    taken = (turned[NB : NB + 1] > 0.5) & (slot < NB)
    place_v[...] = jnp.where(taken, ((col >> 3) << 8) | (((low - slot) & 7) << 4) | low, 15)
    place_copy = pltpu.make_async_copy(place_v, place_s, sem.at[1])
    place_copy.start()
    for a, acc in enumerate(accs):
        acc[...] = jnp.zeros_like(acc)
        count[a] = 0
    place_copy.wait()

    @pl.loop(0, N_GRP)
    def _(src):
        for s in range(SLOTS):
            a, e = s // 2, src * SLOTS + s
            had = count[a]
            listed[a, had] = e
            count[a] = had + jnp.where(place_s[0, e] == 15, 0, 1)

    most = functools.reduce(jnp.maximum, [count[a] for a in range(OWN)])
    for a in range(OWN):

        @pl.loop(count[a], most)
        def _(j):
            listed[a, j] = B

    group = iota((K, B), 1) >> 4

    @pl.loop(0, most)
    def _(j):
        rows = []
        for a in range(OWN):
            code = listed[a, j]
            e = code & (B - 1)
            width = pltpu.roll(widths, (B - e) & (B - 1), 1)[:, :1]
            rows.append((e, (code >> 7) * NB, w[e].astype(I32).astype(F32) * width))
        for n in range(NB):
            for acc, (e, skip, x) in zip(accs, rows):
                place = place_s[n + skip, e]
                acc[place >> 8] += jnp.where(group == (place & 15), pltpu.roll(x, place & 0x70, 1), 0.0)

    for a, acc in enumerate(accs):
        for h in range(CH):
            coarse[a, :, h * B : (h + 1) * B] = acc[h]
    copy.wait()


def on_device(q_blocks, p_blocks, col_index, agg_of_block):
    vmem, hbm, any_ = (pl.BlockSpec(memory_space=m) for m in (pltpu.VMEM, pltpu.HBM, pl.ANY))
    dma = pltpu.SemaphoreType.DMA
    prod, w_in, meta_in = pl.pallas_call(
        product_kernel,
        in_specs=[hbm] * 4,
        out_specs=[vmem, any_, any_],
        out_shape=[
            jax.ShapeDtypeStruct((R, K, B), F32),
            jax.ShapeDtypeStruct((N_GRP, SLOTS, K, B), jnp.int16),
            jax.ShapeDtypeStruct((N_GRP, SLOTS, B), F32),
        ],
        scratch_shapes=[
            pltpu.VMEM((R, NB, B, B), BF16),
            pltpu.VMEM((3 * R, K, B), BF16),
            pltpu.VMEM((2 * R, K, B), BF16),
            pltpu.SMEM((NB, R), I32),
            pltpu.VMEM((NB, R), I32),
            pltpu.VMEM((1, R), I32),
            pltpu.VMEM((5, 8, B), F32),
            pltpu.VMEM((R, B, 2 * B), BF16),
            pltpu.VMEM((R, K, B), jnp.int16),
            pltpu.VMEM((N_GRP, SLOTS, K, B), jnp.int16),
            pltpu.VMEM((B, B), F32),
            pltpu.VMEM((N_GRP, SLOTS, B), F32),
            pltpu.VMEM((8, B), I32),
            pltpu.SMEM((8, B), I32),
            dma((4,)),
            dma((7,)),
            dma((4,)),
            dma((4,)),
            dma((4,)),
            dma((4,)),
            dma((N_GRP,)),
            dma((N_GRP,)),
            dma((N_GRP,)),
            dma((N_GRP,)),
        ],
        compiler_params=pltpu.CompilerParams(
            collective_id=0, has_side_effects=True, vmem_limit_bytes=40 << 20
        ),
        name="products",
    )(col_index.T, agg_of_block.reshape(1, R), q_blocks, p_blocks)
    coarse, product = pl.pallas_call(
        coarse_kernel,
        in_specs=[vmem, vmem, any_],
        out_specs=[vmem, any_],
        out_shape=[
            jax.ShapeDtypeStruct((OWN, K, CH * B), F32),
            jax.ShapeDtypeStruct((R, K, B), F32),
        ],
        scratch_shapes=[pltpu.VMEM((CH, K, B), F32)] * OWN
        + [pltpu.VMEM((K, B), I32), pltpu.SMEM((K, B), I32), pltpu.SMEM((OWN, B), I32), pltpu.SMEM((OWN,), I32)]
        + [dma((2,))],
        compiler_params=pltpu.CompilerParams(vmem_limit_bytes=16 << 20),
        name="coarse",
    )(meta_in.reshape(N_GRP * SLOTS, B), w_in.reshape(N_GRP * SLOTS, K, B), prod)
    return product, coarse


def solution(mesh):
    placed = (
        P(("base", "grp"), None, None, None),
        P(("base", "grp"), None, None),
        P(("base", "grp"), None),
        P(("base", "grp"), None),
    )
    return jax.shard_map(
        on_device,
        mesh=mesh,
        in_specs=placed,
        out_specs=(P(("base", "grp"), None, None), P(("base", "grp"), None, None)),
        check_vma=False,
    )
```

time: 50.9 us -> 44 us (0.86)
  the two profiles are of different devices: /device:TPU:33 before, /device:TPU:40 now
where the time goes in v2:
time: 44 us; the launch traced here: 43.8 us
  Pallas kernels  40.9 us (93%)
  local copies, waits for them, and re-layouts  2.28 us (5%)
  between operations  0.65 us (1%)
    pallas_call x1, Pallas kernels, on_device(): pl.pallas_call(product_kernel, in_specs=[hbm] * 4, out_specs=[vmem, any_,...  29.2 us
    pallas_call x1, Pallas kernels, on_device(): pl.pallas_call(coarse_kernel, in_specs=[vmem, vmem, any_], out_specs=[vme...  11.6 us
    unnamed x6, local copies, waits for them, and re-layouts  2.28 us

profile of v2, /device:TPU:40, one launch (start us, length us, event | category | flops | bytes accessed | tf_op | source)
XLA Modules:
  0.0 43.8 jit_solution(14739813177205724748)
XLA Ops:
  0.6 0.0 copy-start
  0.6 0.9 %copy-done = bf16[64,16,128]{2,1,0:T(8,128)(2,1)S(1)} copy-done((bf16[64,16,128]{2,1,0:T(8,128)(2,1)S(1)}, bf16[64,16,128]{2,1,0:T(8,128)(2,1)}, u32[]{:S(2)}) %copy-start) | copy-done | bytes 262168
  1.6 0.0 copy-start.1
  1.6 0.7 %copy-done.1 = s32[64,8]{0,1:T(8,128)S(1)} copy-done((s32[64,8]{0,1:T(8,128)S(1)}, s32[64,8]{0,1:T(8,128)}, u32[]{:S(2)}) %copy-start.1) | copy-done | bytes 2072
  2.3 0.0 copy-start.2
  2.3 0.7 %copy-done.2 = s32[64,1]{0,1:T(1,128)S(1)} copy-done((s32[64,1]{0,1:T(1,128)S(1)}, s32[64,1]{0,1:T(1,128)}, u32[]{:S(2)}) %copy-start.2) | copy-done | bytes 280
  2.9 29.2 %products.1 = (f32[64,16,128]{2,1,0:T(8,128)S(1)}, s16[16,8,16,128]{3,2,1,0:T(8,128)(2,1)S(1)}, f32[16,8,128]{2,1,0:T(8,128)S(1)}) custom-call(s32[8,64]{1,0:T(8,128)S(1)} %bitcast.6, s32[1,64]{1,0:T(1,128)S(1)} %bitcast.7, bf16[64,8,128,128]{3,2,1,0:T(8,128)(2,1)} %q_hbm.1, bf16[64,16,128]{2,1,0:T(8,128)(2,1)S(1)} %copy-done), custom_call_target="tpu_custom_call" | custom-call | tf_op jit(solution)/shard_map/products/pallas_call | solution.py:274
  32.2 11.6 %coarse.1 = (f32[4,16,3072]{2,1,0:T(8,128)}, f32[64,16,128]{2,1,0:T(8,128)}) custom-call(f32[128,128]{1,0:T(8,128)S(1)} %bitcast.5, s16[128,16,128]{2,1,0:T(8,128)(2,1)S(1)} %bitcast.4, f32[64,16,128]{2,1,0:T(8,128)S(1)} %get-tuple-element.9.prod_in), custom_call_target="tpu_custom_call" | custom-call | tf_op jit(solution)/shard_map/coarse/pallas_call | solution.py:314
Async XLA Ops:
  0.6 1.0 %copy-start = (bf16[64,16,128]{2,1,0:T(8,128)(2,1)S(1)}, bf16[64,16,128]{2,1,0:T(8,128)(2,1)}, u32[]{:S(2)}) copy-start(bf16[64,16,128]{2,1,0:T(8,128)(2,1)} %p_hbm.1) | copy-start | bytes 786436
  1.6 0.7 %copy-start.1 = (s32[64,8]{0,1:T(8,128)S(1)}, s32[64,8]{0,1:T(8,128)}, u32[]{:S(2)}) copy-start(s32[64,8]{0,1:T(8,128)} %param.6) | copy-start | bytes 6148
  2.3 0.7 %copy-start.2 = (s32[64,1]{0,1:T(1,128)S(1)}, s32[64,1]{0,1:T(1,128)}, u32[]{:S(2)}) copy-start(s32[64,1]{0,1:T(1,128)} %param.7) | copy-start | bytes 772

commit v3 on v2

--- a/solution.py
+++ b/solution.py
@@ -213,54 +213,40 @@
 
 
 def coarse_kernel(
-    meta, w, prod_in, coarse, prod_out, acc0, acc1, acc2, acc3, place_v, place_s, listed, count, sem
+    meta, w, prod_in, coarse, prod_out, acc0, acc1, acc2, acc3, rows, chunk_v, turn_v, chunk, turn, sem
 ):
     copy = pltpu.make_async_copy(prod_in, prod_out, sem.at[0])
     copy.start()
     accs = (acc0, acc1, acc2, acc3)
     turned = meta[...].T
-    widths = turned[K : 2 * K] * (1.0 / STEPS)
-    slot = iota((K, B), 0)
-    col = turned[:K].astype(I32)
-    low = col & 7
-    taken = (turned[NB : NB + 1] > 0.5) & (slot < NB)
-    place_v[...] = jnp.where(taken, ((col >> 3) << 8) | (((low - slot) & 7) << 4) | low, 15)
-    place_copy = pltpu.make_async_copy(place_v, place_s, sem.at[1])
-    place_copy.start()
-    for a, acc in enumerate(accs):
+    taken = turned[NB : NB + 1] > 0.5
+    col = jnp.where(taken, turned[:NB], 0.0).astype(I32)
+    chunk_v[...] = col >> 3
+    turn_v[...] = (((col & 7) - iota((NB, B), 0)) & 7) * K
+    place_copies = [
+        pltpu.make_async_copy(src, dst, sem.at[s]) for src, dst, s in ((chunk_v, chunk, 1), (turn_v, turn, 2))
+    ]
+    for c in place_copies:
+        c.start()
+    for acc in accs:
         acc[...] = jnp.zeros_like(acc)
-        count[a] = 0
-    place_copy.wait()
-
-    @pl.loop(0, N_GRP)
-    def _(src):
-        for s in range(SLOTS):
-            a, e = s // 2, src * SLOTS + s
-            had = count[a]
-            listed[a, had] = e
-            count[a] = had + jnp.where(place_s[0, e] == 15, 0, 1)
-
-    most = functools.reduce(jnp.maximum, [count[a] for a in range(OWN)])
-    for a in range(OWN):
-
-        @pl.loop(count[a], most)
-        def _(j):
-            listed[a, j] = B
+    widths = jnp.where(taken, turned[K : 2 * K] * (1.0 / STEPS), 0.0)
+    for e in range(B):
+        rows[e] = w[e].astype(I32).astype(F32) * widths[:, e : e + 1]
+    for c in place_copies:
+        c.wait()
 
     group = iota((K, B), 1) >> 4
 
-    @pl.loop(0, most)
+    @pl.loop(0, N_GRP // 4)
     def _(j):
-        rows = []
-        for a in range(OWN):
-            code = listed[a, j]
-            e = code & (B - 1)
-            width = pltpu.roll(widths, (B - e) & (B - 1), 1)[:, :1]
-            rows.append((e, (code >> 7) * NB, w[e].astype(I32).astype(F32) * width))
-        for n in range(NB):
-            for acc, (e, skip, x) in zip(accs, rows):
-                place = place_s[n + skip, e]
-                acc[place >> 8] += jnp.where(group == (place & 15), pltpu.roll(x, place & 0x70, 1), 0.0)
+        for u in range(4):
+            for t in range(2):
+                for n in range(NB):
+                    for a, acc in enumerate(accs):
+                        e = j * (4 * SLOTS) + (u * SLOTS + 2 * a + t)
+                        one = jnp.where(group == n, rows[e], 0.0)
+                        acc[chunk[n, e]] += pltpu.roll(one, turn[n, e], 1)
 
     for a, acc in enumerate(accs):
         for h in range(CH):
@@ -271,6 +257,7 @@
 def on_device(q_blocks, p_blocks, col_index, agg_of_block):
     vmem, hbm, any_ = (pl.BlockSpec(memory_space=m) for m in (pltpu.VMEM, pltpu.HBM, pl.ANY))
     dma = pltpu.SemaphoreType.DMA
+    inputs = (col_index.T, agg_of_block.reshape(1, R), q_blocks, p_blocks)
     prod, w_in, meta_in = pl.pallas_call(
         product_kernel,
         in_specs=[hbm] * 4,
@@ -310,7 +297,7 @@
             collective_id=0, has_side_effects=True, vmem_limit_bytes=40 << 20
         ),
         name="products",
-    )(col_index.T, agg_of_block.reshape(1, R), q_blocks, p_blocks)
+    )(*(pltpu.with_memory_space_constraint(x, pltpu.HBM) for x in inputs))
     coarse, product = pl.pallas_call(
         coarse_kernel,
         in_specs=[vmem, vmem, any_],
@@ -320,8 +307,10 @@
             jax.ShapeDtypeStruct((R, K, B), F32),
         ],
         scratch_shapes=[pltpu.VMEM((CH, K, B), F32)] * OWN
-        + [pltpu.VMEM((K, B), I32), pltpu.SMEM((K, B), I32), pltpu.SMEM((OWN, B), I32), pltpu.SMEM((OWN,), I32)]
-        + [dma((2,))],
+        + [pltpu.VMEM((B, K, B), F32)]
+        + [pltpu.VMEM((NB, B), I32)] * 2
+        + [pltpu.SMEM((NB, B), I32)] * 2
+        + [dma((3,))],
         compiler_params=pltpu.CompilerParams(vmem_limit_bytes=16 << 20),
         name="coarse",
     )(meta_in.reshape(N_GRP * SLOTS, B), w_in.reshape(N_GRP * SLOTS, K, B), prod)

time: 44 us -> 36.2 us (0.82)
  the two profiles are of different devices: /device:TPU:40 before, /device:TPU:33 now
where the time goes in v3:
time: 36.2 us; the launch traced here: 35.6 us
  Pallas kernels  35 us (97%)
  between operations  0.64 us (2%)
    pallas_call x1, Pallas kernels, on_device(): pl.pallas_call(product_kernel, in_specs=[hbm] * 4, out_specs=[vmem, any_,...  30.3 us
    pallas_call x1, Pallas kernels, on_device(): pl.pallas_call(coarse_kernel, in_specs=[vmem, vmem, any_], out_specs=[vme...  4.64 us

profile of v3, /device:TPU:33, one launch (start us, length us, event | category | flops | bytes accessed | tf_op | source)
XLA Modules:
  0.0 35.6 jit_solution(2955372412890702239)
XLA Ops:
  0.6 30.3 %products.1 = (f32[64,16,128]{2,1,0:T(8,128)S(1)}, s16[16,8,16,128]{3,2,1,0:T(8,128)(2,1)S(1)}, f32[16,8,128]{2,1,0:T(8,128)S(1)}) custom-call(s32[8,64]{1,0:T(8,128)} %bitcast.6, s32[1,64]{1,0:T(1,128)} %bitcast.7, bf16[64,8,128,128]{3,2,1,0:T(8,128)(2,1)} %q_hbm.1, bf16[64,16,128]{2,1,0:T(8,128)(2,1)} %p_hbm.1), custom_call_target="tpu_custom_call" | custom-call | tf_op jit(solution)/shard_map/products/pallas_call | solution.py:261
  31.0 4.6 %coarse.1 = (f32[4,16,3072]{2,1,0:T(8,128)}, f32[64,16,128]{2,1,0:T(8,128)}) custom-call(f32[128,128]{1,0:T(8,128)S(1)} %bitcast.5, s16[128,16,128]{2,1,0:T(8,128)(2,1)S(1)} %bitcast.4, f32[64,16,128]{2,1,0:T(8,128)S(1)} %get-tuple-element.9.prod_in), custom_call_target="tpu_custom_call" | custom-call | tf_op jit(solution)/shard_map/coarse/pallas_call | solution.py:301

commit v4 on v3

v4 whole, which is shorter than its diff:
```python
import functools

import jax
import jax.numpy as jnp
from jax import lax
from jax.experimental import pallas as pl
from jax.experimental.pallas import tpu as pltpu
from jax.sharding import PartitionSpec as P

F32, BF16, I32 = jnp.float32, jnp.bfloat16, jnp.int32
MESH = pl.DeviceIdType.MESH
R, NB, NB_IN, K, B = 64, 8, 6, 16, 128
N_BASE, N_GRP = 8, 16
OWN = 4
SLOTS = 2 * OWN
STEPS = 32000.0
CH = 24
SIDE = 4
STEPS_TO = sorted(
    ((dy, dx) for dy in range(SIDE) for dx in range(SIDE)),
    key=lambda d: (-min(d[0], SIDE - d[0]) - min(d[1], SIDE - d[1]), d),
)[:-1]
EARLY, LATE = ((0,),), ((1, 2), (3, 4), (6, 7), (5,))


def dot_t(a, b):
    return lax.dot_general(a, b, (((1,), (1,)), ((), ())), preferred_element_type=F32)


def iota(shape, dim):
    return lax.broadcasted_iota(I32, shape, dim)


def product_kernel(
    col_hbm, agg_hbm, q_hbm, p_hbm,
    prod, w_in,
    q_v, near, side, col_s, col_v, agg_v, aggtab, split, w_v, pack, info, order_v, order_s,
    q_sem, loc_sem, p_send, p_recv, a_send, a_recv, w_send, w_recv,
):
    base, grp = lax.axis_index("base"), lax.axis_index("grp")
    barrier = pltpu.get_barrier_semaphore()
    for d in range(1, N_GRP):
        pl.semaphore_signal(barrier, 1, device_id={"grp": (grp + d) % N_GRP}, device_id_type=MESH)
    for d in (1, N_BASE - 1):
        pl.semaphore_signal(barrier, 1, device_id={"base": (base + d) % N_BASE}, device_id_type=MESH)
    sends = (
        ({"grp": (grp + 1) % N_GRP}, near, 0, 0),
        ({"grp": (grp + N_GRP - 1) % N_GRP}, near, 2, 2),
        ({"base": (base + 1) % N_BASE}, side, 0, 3),
        ({"base": (base + N_BASE - 1) % N_BASE}, side, 1, 4),
    )
    agg_copy = pltpu.make_async_copy(agg_hbm, agg_v, loc_sem.at[0])
    col_copies = (
        pltpu.make_async_copy(col_hbm, col_s, loc_sem.at[1]),
        pltpu.make_async_copy(col_hbm, col_v, loc_sem.at[2]),
    )
    own_copy = pltpu.make_async_copy(p_hbm, near.at[pl.ds(R, R)], loc_sem.at[3])
    for c in (agg_copy, *col_copies, own_copy):
        c.start()
    q_copies = [
        pltpu.make_async_copy(q_hbm.at[:, pl.ds(a, size)], q_v.at[:, pl.ds(a, size)], q_sem.at[c])
        for c, (a, size) in enumerate(((0, 1), (1, 5), (6, 2)))
    ]
    for c in q_copies[:1]:
        c.start()

    row, lane = iota((R, B), 0), iota((R, B), 1)
    agg_copy.wait()
    agg_row = jnp.concatenate([agg_v[...], jnp.zeros((1, B - R), I32)], 1).astype(F32)
    aggtab[1] = jnp.broadcast_to(agg_row, (8, B))

    pl.semaphore_wait(barrier, N_GRP + 1)
    p_copies, a_copies = [], []
    for s, (to, tab, part, seg) in enumerate(sends):
        p_copies.append(
            pltpu.make_async_remote_copy(
                p_hbm, tab.at[pl.ds(part * R, R)], p_send.at[s], p_recv.at[s], device_id=to, device_id_type=MESH
            )
        )
        a_copies.append(
            pltpu.make_async_remote_copy(
                aggtab.at[1], aggtab.at[seg], a_send.at[s], a_recv.at[s], device_id=to, device_id_type=MESH
            )
        )
    for c in a_copies + p_copies:
        c.start()
    for c in q_copies[1:]:
        c.start()

    agg_col = jnp.sum(jnp.where(row == lane, agg_row, 0.0), axis=1, keepdims=True)
    before = (agg_col == agg_row) & (lane < row)
    rank = jnp.sum(jnp.where(before, 1.0, 0.0), axis=1, keepdims=True)
    match = (2.0 * agg_col + rank) == lane.astype(F32)
    order = jnp.sum(jnp.where(match, row.astype(F32), 0.0), axis=0, keepdims=True)
    order_v[...] = jnp.broadcast_to(order, (8, B)).astype(I32)
    order_copy = pltpu.make_async_copy(order_v, order_s, loc_sem.at[4])
    order_copy.start()

    def position(c, slot):
        if slot >= NB_IN:
            return (c >> 11) * R + (c & (R - 1))
        shard = jnp.minimum(((c >> 6) - grp + 1) & (N_GRP - 1), 2)
        return shard * R + (c & (R - 1))

    def block_of(i, n):
        if n == 0:
            return near[R + i]
        return (side if n >= NB_IN else near)[position(col_s[n, i], n)]

    def values(blocks):
        zero = jnp.zeros((K, B), BF16)
        rows = [block_of(*b) for b in blocks]
        lhs = jnp.concatenate(
            [jnp.concatenate([x, zero] if e % 2 == 0 else [zero, x], 1) for e, x in enumerate(rows)], 0
        )
        rhs = jnp.concatenate([jnp.concatenate([q_v[b] for b in blocks[e : e + 2]], 1) for e in (0, 2)], 0)
        out = dot_t(lhs, rhs)
        parts = []
        for e, (i, n) in enumerate(blocks):
            v = out[e * K : (e + 1) * K, e // 2 * B : (e // 2 + 1) * B]
            high = v.astype(BF16)
            split[i, n * K : (n + 1) * K, :B] = high
            split[i, n * K : (n + 1) * K, B:] = (v - high.astype(F32)).astype(BF16)
            parts.append(v)
        return parts

    def four_rows(i, slots):
        sums = [[], [], [], []]
        for group in slots:
            if len(group) == 1:
                sets = [[(d, group[0]) for d in range(4)]]
            else:
                sets = [[(d + e, n) for e in range(2) for n in group] for d in (0, 2)]
            for blocks in sets:
                for (d, _), v in zip(blocks, values([(i + d, n) for d, n in blocks])):
                    sums[d].append(v)
        return [functools.reduce(jnp.add, parts) for parts in sums]

    for c in col_copies:
        c.wait()
    for c in a_copies:
        c.wait_recv()
    col = jnp.concatenate([col_v[...], jnp.zeros((NB, B - R), I32)], 1)
    near_at, side_at = position(col, 0), position(col, NB_IN)

    def looked_up(low, high, at):
        table = jnp.concatenate([aggtab[low][:, :R], aggtab[high][:, :R]], 1)
        return jnp.take_along_axis(table, at, axis=1)

    inner = jnp.where(near_at < B, looked_up(0, 1, near_at & (B - 1)), looked_up(2, 2, near_at & (B - 1)))
    outer = looked_up(3, 4, side_at & (B - 1))
    colagg = jnp.where(iota((NB, B), 0) < NB_IN, inner, outer) + ((col >> 10) * R).astype(F32)
    ones = jnp.where(iota((K - NB, B), 0) == 0, 1.0, 0.0)
    by_row = jnp.concatenate([colagg, ones], 0).astype(BF16)
    info[...] = jnp.dot(by_row[:, :R], jnp.where(match, 1.0, 0.0).astype(BF16), preferred_element_type=F32)

    own_copy.wait()
    q_copies[0].wait()

    @pl.loop(0, R // 16)
    def _(j):
        for u in range(0, 16, 4):
            i = j * 16 + u
            for d, v in enumerate(four_rows(i, EARLY)):
                prod[i + d] = v

    for c in p_copies:
        c.wait_recv()
    for c in q_copies[1:]:
        c.wait()

    @pl.loop(0, R // 16)
    def _(j):
        for u in range(0, 16, 4):
            i = j * 16 + u
            for d, v in enumerate(four_rows(i, LATE)):
                prod[i + d] += v

    order_copy.wait()

    def weights(to, half):
        for t in range(0, SLOTS, 2):
            two = [order_s[0, to * SLOTS + t + d] & (R - 1) for d in range(2)]
            p_two = jnp.concatenate([near[R + i] for i in two], 0)
            out = dot_t(jnp.concatenate([p_two, p_two], 1), jnp.concatenate([split[i] for i in two], 0))
            w_v[half, t] = out[:K, :B]
            w_v[half, t + 1] = out[K:, B:]

    def coded(to, half):
        tile = pltpu.roll(info[...], (B + SLOTS - SLOTS * to) % B, 1)
        for t in range(SLOTS):
            w = w_v[half, t]
            most = jnp.maximum(jnp.max(jnp.abs(w), axis=1, keepdims=True), 1e-30)
            width = jnp.ceil(2.0 * jnp.log2(most) + 0.02)
            pack[to, t] = jnp.round(w * (STEPS / jnp.exp2(0.5 * width))).astype(I32).astype(jnp.int16)
            tile = jnp.where(spot == t, width, tile)
        pack[to, SLOTS] = tile.astype(I32).astype(jnp.int16)

    spot = iota((K, B), 1)
    y, x = grp // SIDE, grp % SIDE
    owners = [(y + dy) % SIDE * SIDE + (x + dx) % SIDE for dy, dx in STEPS_TO] + [grp]
    copies = []
    weights(owners[0], 0)
    for s, to in enumerate(owners):
        if s + 1 < N_GRP:
            weights(owners[s + 1], (s + 1) % 2)
        coded(to, s % 2)
        if s + 1 < N_GRP:
            copies.append(
                pltpu.make_async_remote_copy(
                    pack.at[to], w_in.at[grp], w_send.at[s], w_recv.at[s], device_id={"grp": to}, device_id_type=MESH
                )
            )
        else:
            copies.append(pltpu.make_async_copy(pack.at[to], w_in.at[grp], loc_sem.at[5]))
        copies[-1].start()
    for c in p_copies + a_copies:
        c.wait_send()
    for c in copies:
        c.wait()


def coarse_kernel(
    w, prod_in, coarse, prod_out, acc0, acc1, acc2, acc3, rows, chunk_v, turn_v, chunk, turn, sem
):
    copy = pltpu.make_async_copy(prod_in, prod_out, sem.at[0])
    copy.start()
    accs = (acc0, acc1, acc2, acc3)
    owner_of = iota((K, B), 1) // SLOTS
    widths, cols = jnp.zeros((K, B), F32), jnp.zeros((K, B), F32)
    for src in range(N_GRP):
        tile = w[src, SLOTS].astype(I32).astype(F32)
        widths = jnp.where(owner_of == src, pltpu.roll(tile, src * SLOTS, 1), widths)
        cols = jnp.where(owner_of == src, pltpu.roll(tile, (src + N_GRP - 1) % N_GRP * SLOTS, 1), cols)
    taken = cols[NB : NB + 1] > 0.5
    col = jnp.where(taken, cols[:NB], 0.0).astype(I32)
    chunk_v[...] = col >> 3
    turn_v[...] = (((col & 7) - iota((NB, B), 0)) & 7) * K
    place_copies = [
        pltpu.make_async_copy(src, dst, sem.at[s]) for src, dst, s in ((chunk_v, chunk, 1), (turn_v, turn, 2))
    ]
    for c in place_copies:
        c.start()
    for acc in accs:
        acc[...] = jnp.zeros_like(acc)
    widths = jnp.where(taken, jnp.exp2(0.5 * widths) * (1.0 / STEPS), 0.0)
    for e in range(B):
        rows[e] = w[e // SLOTS, e % SLOTS].astype(I32).astype(F32) * widths[:, e : e + 1]
    for c in place_copies:
        c.wait()

    group = iota((K, B), 1) >> 4

    @pl.loop(0, N_GRP // 4)
    def _(j):
        for u in range(4):
            for t in range(2):
                for n in range(NB):
                    for a, acc in enumerate(accs):
                        e = j * (4 * SLOTS) + (u * SLOTS + 2 * a + t)
                        one = jnp.where(group == n, rows[e], 0.0)
                        acc[chunk[n, e]] += pltpu.roll(one, turn[n, e], 1)

    for a, acc in enumerate(accs):
        for h in range(CH):
            coarse[a, :, h * B : (h + 1) * B] = acc[h]
    copy.wait()


def on_device(q_blocks, p_blocks, col_index, agg_of_block):
    vmem, hbm, any_ = (pl.BlockSpec(memory_space=m) for m in (pltpu.VMEM, pltpu.HBM, pl.ANY))
    dma = pltpu.SemaphoreType.DMA
    inputs = (col_index.T, agg_of_block.reshape(1, R), q_blocks, p_blocks)
    prod, w_in = pl.pallas_call(
        product_kernel,
        in_specs=[hbm] * 4,
        out_specs=[vmem, any_],
        out_shape=[
            jax.ShapeDtypeStruct((R, K, B), F32),
            jax.ShapeDtypeStruct((N_GRP, SLOTS + 1, K, B), jnp.int16),
        ],
        scratch_shapes=[
            pltpu.VMEM((R, NB, B, B), BF16),
            pltpu.VMEM((3 * R, K, B), BF16),
            pltpu.VMEM((2 * R, K, B), BF16),
            pltpu.SMEM((NB, R), I32),
            pltpu.VMEM((NB, R), I32),
            pltpu.VMEM((1, R), I32),
            pltpu.VMEM((5, 8, B), F32),
            pltpu.VMEM((R, B, 2 * B), BF16),
            pltpu.VMEM((2, SLOTS, K, B), F32),
            pltpu.VMEM((N_GRP, SLOTS + 1, K, B), jnp.int16),
            pltpu.VMEM((K, B), F32),
            pltpu.VMEM((8, B), I32),
            pltpu.SMEM((8, B), I32),
            dma((3,)),
            dma((6,)),
            dma((4,)),
            dma((4,)),
            dma((4,)),
            dma((4,)),
            dma((N_GRP,)),
            dma((N_GRP,)),
        ],
        compiler_params=pltpu.CompilerParams(
            collective_id=0, has_side_effects=True, vmem_limit_bytes=40 << 20
        ),
        name="products",
    )(*(pltpu.with_memory_space_constraint(x, pltpu.HBM) for x in inputs))
    coarse, product = pl.pallas_call(
        coarse_kernel,
        in_specs=[vmem, any_],
        out_specs=[vmem, any_],
        out_shape=[
            jax.ShapeDtypeStruct((OWN, K, CH * B), F32),
            jax.ShapeDtypeStruct((R, K, B), F32),
        ],
        scratch_shapes=[pltpu.VMEM((CH, K, B), F32)] * OWN
        + [pltpu.VMEM((B, K, B), F32)]
        + [pltpu.VMEM((NB, B), I32)] * 2
        + [pltpu.SMEM((NB, B), I32)] * 2
        + [dma((3,))],
        compiler_params=pltpu.CompilerParams(vmem_limit_bytes=16 << 20),
        name="coarse",
    )(w_in, prod)
    return product, coarse


def solution(mesh):
    placed = (
        P(("base", "grp"), None, None, None),
        P(("base", "grp"), None, None),
        P(("base", "grp"), None),
        P(("base", "grp"), None),
    )
    return jax.shard_map(
        on_device,
        mesh=mesh,
        in_specs=placed,
        out_specs=(P(("base", "grp"), None, None), P(("base", "grp"), None, None)),
        check_vma=False,
    )
```

time: 36.2 us -> 33.9 us (0.936); the launches traced: 35.6 us -> 33.8 us
  Pallas kernels: 35 us -> 33.1 us
    pallas_call x2, Pallas kernels: 35 us -> 33.1 us  [the longest x1 28.5 us: on_device(): pl.pallas_call(product_kernel, in_specs=[hbm] * 4, out_specs=[vmem, any_]...]
where the time goes in v4:
time: 33.9 us; the launch traced here: 33.8 us
  Pallas kernels  33.1 us (98%)
  between operations  0.64 us (2%)
    pallas_call x1, Pallas kernels, on_device(): pl.pallas_call(product_kernel, in_specs=[hbm] * 4, out_specs=[vmem, any_]...  28.5 us
    pallas_call x1, Pallas kernels, on_device(): pl.pallas_call(coarse_kernel, in_specs=[vmem, any_], out_specs=[vmem, any...  4.69 us

profile of v4, /device:TPU:33, one launch (start us, length us, event | category | flops | bytes accessed | tf_op | source)
XLA Modules:
  0.0 33.8 jit_solution(14156401368688132328)
XLA Ops:
  0.6 28.5 %products.1 = (f32[64,16,128]{2,1,0:T(8,128)S(1)}, s16[16,9,16,128]{3,2,1,0:T(8,128)(2,1)S(1)}) custom-call(s32[8,64]{1,0:T(8,128)} %bitcast.2, s32[1,64]{1,0:T(1,128)} %bitcast.3, bf16[64,8,128,128]{3,2,1,0:T(8,128)(2,1)} %q_hbm.1, bf16[64,16,128]{2,1,0:T(8,128)(2,1)} %p_hbm.1), custom_call_target="tpu_custom_call" | custom-call | tf_op jit(solution)/shard_map/products/pallas_call | solution.py:274
  29.1 4.7 %coarse.1 = (f32[4,16,3072]{2,1,0:T(8,128)}, f32[64,16,128]{2,1,0:T(8,128)}) custom-call(s16[16,9,16,128]{3,2,1,0:T(8,128)(2,1)S(1)} %get-tuple-element.6.w, f32[64,16,128]{2,1,0:T(8,128)S(1)} %get-tuple-element.7.prod_in), custom_call_target="tpu_custom_call" | custom-call | tf_op jit(solution)/shard_map/coarse/pallas_call | solution.py:310

commit v5 on v4

--- a/solution.py
+++ b/solution.py
@@ -34,7 +34,7 @@
 def product_kernel(
     col_hbm, agg_hbm, q_hbm, p_hbm,
     prod, w_in,
-    q_v, near, side, col_s, col_v, agg_v, aggtab, split, w_v, pack, info, order_v, order_s,
+    q_v, near, side, col_s, col_v, agg_v, aggtab, split, w_v, pack, info, order_v, order_s, first, prod_v,
     q_sem, loc_sem, p_send, p_recv, a_send, a_recv, w_send, w_recv,
 ):
     base, grp = lax.axis_index("base"), lax.axis_index("grp")
@@ -90,9 +90,29 @@
     agg_col = jnp.sum(jnp.where(row == lane, agg_row, 0.0), axis=1, keepdims=True)
     before = (agg_col == agg_row) & (lane < row)
     rank = jnp.sum(jnp.where(before, 1.0, 0.0), axis=1, keepdims=True)
-    match = (2.0 * agg_col + rank) == lane.astype(F32)
-    order = jnp.sum(jnp.where(match, row.astype(F32), 0.0), axis=0, keepdims=True)
-    order_v[...] = jnp.broadcast_to(order, (8, B)).astype(I32)
+    y, x = grp // SIDE, grp % SIDE
+    agg_int = agg_col.astype(I32)
+    step = (((agg_int >> 4) - y) & (SIDE - 1)) * SIDE + (((agg_int >> 2) - x) & (SIDE - 1))
+    turn = jnp.full((R, 1), 1.0 * len(STEPS_TO), F32)
+    for s, (dy, dx) in enumerate(STEPS_TO):
+        turn = jnp.where(step == dy * SIDE + dx, 1.0 * s, turn)
+    place = SLOTS * turn + 2.0 * (agg_int & (OWN - 1)).astype(F32) + rank
+
+    def across(taken, value):
+        return jnp.sum(jnp.where(taken, value, 0.0), axis=0, keepdims=True)
+
+    row_f, lane_f = row.astype(F32), lane.astype(F32)
+    match = place == lane_f
+    ahead = (across(row == lane, place) < place) & (lane < R)
+    position_of = jnp.sum(jnp.where(ahead, 1.0, 0.0), axis=1, keepdims=True)
+    lists = [
+        across(match, row_f),
+        across(match, position_of),
+        across(position_of == lane_f, row_f),
+        across(row == lane, position_of),
+        jnp.zeros((4, B), F32),
+    ]
+    order_v[...] = jnp.concatenate(lists, 0).astype(I32)
     order_copy = pltpu.make_async_copy(order_v, order_s, loc_sem.at[4])
     order_copy.start()
 
@@ -109,22 +129,29 @@
 
     def values(blocks):
         zero = jnp.zeros((K, B), BF16)
-        rows = [block_of(*b) for b in blocks]
+        rows = [block_of(i, n) for i, n, _ in blocks]
         lhs = jnp.concatenate(
-            [jnp.concatenate([x, zero] if e % 2 == 0 else [zero, x], 1) for e, x in enumerate(rows)], 0
+            [jnp.concatenate([v, zero] if e % 2 == 0 else [zero, v], 1) for e, v in enumerate(rows)], 0
         )
-        rhs = jnp.concatenate([jnp.concatenate([q_v[b] for b in blocks[e : e + 2]], 1) for e in (0, 2)], 0)
+        rhs = jnp.concatenate(
+            [jnp.concatenate([q_v[i, n] for i, n, _ in blocks[e : e + 2]], 1) for e in (0, 2)], 0
+        )
         out = dot_t(lhs, rhs)
         parts = []
-        for e, (i, n) in enumerate(blocks):
+        for e, (_, n, at) in enumerate(blocks):
             v = out[e * K : (e + 1) * K, e // 2 * B : (e // 2 + 1) * B]
             high = v.astype(BF16)
-            split[i, n * K : (n + 1) * K, :B] = high
-            split[i, n * K : (n + 1) * K, B:] = (v - high.astype(F32)).astype(BF16)
+            low = (v - high.astype(F32)).astype(BF16)
+            if n == 0:
+                first[at, :, :B] = high
+                first[at, :, B:] = low
+            else:
+                split[at, (n - 1) * K : n * K, :B] = high
+                split[at, (n - 1) * K : n * K, B:] = low
             parts.append(v)
         return parts
 
-    def four_rows(i, slots):
+    def four_rows(rows, ats, slots):
         sums = [[], [], [], []]
         for group in slots:
             if len(group) == 1:
@@ -132,7 +159,7 @@
             else:
                 sets = [[(d + e, n) for e in range(2) for n in group] for d in (0, 2)]
             for blocks in sets:
-                for (d, _), v in zip(blocks, values([(i + d, n) for d, n in blocks])):
+                for (d, _), v in zip(blocks, values([(rows[d], n, ats[d]) for d, n in blocks])):
                     sums[d].append(v)
         return [functools.reduce(jnp.add, parts) for parts in sums]
 
@@ -161,7 +188,8 @@
     def _(j):
         for u in range(0, 16, 4):
             i = j * 16 + u
-            for d, v in enumerate(four_rows(i, EARLY)):
+            four = [i + d for d in range(4)]
+            for d, v in enumerate(four_rows(four, four, EARLY)):
                 prod[i + d] = v
 
     for c in p_copies:
@@ -169,51 +197,76 @@
     for c in q_copies[1:]:
         c.wait()
 
-    @pl.loop(0, R // 16)
-    def _(j):
+    order_copy.wait()
+
+    def late(c):
         for u in range(0, 16, 4):
-            i = j * 16 + u
-            for d, v in enumerate(four_rows(i, LATE)):
-                prod[i + d] += v
-
-    order_copy.wait()
-
-    def weights(to, half):
+            ats = [c * 16 + u + d for d in range(4)]
+            rows = [order_s[2, at] & (R - 1) for at in ats]
+            for at, v in zip(ats, four_rows(rows, ats, LATE)):
+                prod_v[at] = v
+
+    def weights(s):
         for t in range(0, SLOTS, 2):
-            two = [order_s[0, to * SLOTS + t + d] & (R - 1) for d in range(2)]
-            p_two = jnp.concatenate([near[R + i] for i in two], 0)
-            out = dot_t(jnp.concatenate([p_two, p_two], 1), jnp.concatenate([split[i] for i in two], 0))
-            w_v[half, t] = out[:K, :B]
-            w_v[half, t + 1] = out[K:, B:]
-
-    def coded(to, half):
-        tile = pltpu.roll(info[...], (B + SLOTS - SLOTS * to) % B, 1)
+            p_two, v_two = [], []
+            for e in (s * SLOTS + t, s * SLOTS + t + 1):
+                i = order_s[0, e] & (R - 1)
+                p_two.append(near[R + i])
+                v_two += [first[i], split[order_s[1, e] & (R - 1)]]
+            p_two = jnp.concatenate(p_two, 0)
+            out = dot_t(jnp.concatenate([p_two, p_two], 1), jnp.concatenate(v_two, 0))
+            w_v[s % 2, t] = out[:K, :B]
+            w_v[s % 2, t + 1] = out[K:, B:]
+
+    def coded(s):
+        tile = pltpu.roll(info[...], (B + SLOTS - SLOTS * s) % B, 1)
         for t in range(SLOTS):
-            w = w_v[half, t]
+            w = w_v[s % 2, t]
             most = jnp.maximum(jnp.max(jnp.abs(w), axis=1, keepdims=True), 1e-30)
             width = jnp.ceil(2.0 * jnp.log2(most) + 0.02)
-            pack[to, t] = jnp.round(w * (STEPS / jnp.exp2(0.5 * width))).astype(I32).astype(jnp.int16)
+            pack[s, t] = jnp.round(w * (STEPS / jnp.exp2(0.5 * width))).astype(I32).astype(jnp.int16)
             tile = jnp.where(spot == t, width, tile)
-        pack[to, SLOTS] = tile.astype(I32).astype(jnp.int16)
-
-    spot = iota((K, B), 1)
-    y, x = grp // SIDE, grp % SIDE
-    owners = [(y + dy) % SIDE * SIDE + (x + dx) % SIDE for dy, dx in STEPS_TO] + [grp]
+        pack[s, SLOTS] = tile.astype(I32).astype(jnp.int16)
+
     copies = []
-    weights(owners[0], 0)
-    for s, to in enumerate(owners):
-        if s + 1 < N_GRP:
-            weights(owners[s + 1], (s + 1) % 2)
-        coded(to, s % 2)
-        if s + 1 < N_GRP:
-            copies.append(
-                pltpu.make_async_remote_copy(
-                    pack.at[to], w_in.at[grp], w_send.at[s], w_recv.at[s], device_id={"grp": to}, device_id_type=MESH
-                )
+
+    def send(s):
+        if s < len(STEPS_TO):
+            dy, dx = STEPS_TO[s]
+            to = (y + dy) % SIDE * SIDE + (x + dx) % SIDE
+            copy = pltpu.make_async_remote_copy(
+                pack.at[s], w_in.at[grp], w_send.at[s], w_recv.at[s], device_id={"grp": to}, device_id_type=MESH
             )
         else:
-            copies.append(pltpu.make_async_copy(pack.at[to], w_in.at[grp], loc_sem.at[5]))
-        copies[-1].start()
+            copy = pltpu.make_async_copy(pack.at[s], w_in.at[grp], loc_sem.at[5])
+        copy.start()
+        copies.append(copy)
+
+    spot = iota((K, B), 1)
+    late(0)
+    for c in range(1, R // 16):
+        two = (2 * c - 2, 2 * c - 1)
+        for s in two:
+            weights(s)
+        late(c)
+        for s in two:
+            coded(s)
+        for s in two:
+            send(s)
+    begin = R // 8 - 2
+    weights(begin)
+    for s in range(begin, N_GRP):
+        if s + 1 < N_GRP:
+            weights(s + 1)
+        coded(s)
+        send(s)
+
+    @pl.loop(0, R // 8)
+    def _(j):
+        for u in range(8):
+            i = j * 8 + u
+            prod[i] += prod_v[order_s[3, i] & (R - 1)]
+
     for c in p_copies + a_copies:
         c.wait_send()
     for c in copies:
@@ -287,12 +340,14 @@
             pltpu.VMEM((NB, R), I32),
             pltpu.VMEM((1, R), I32),
             pltpu.VMEM((5, 8, B), F32),
-            pltpu.VMEM((R, B, 2 * B), BF16),
+            pltpu.VMEM((R, (NB - 1) * K, 2 * B), BF16),
             pltpu.VMEM((2, SLOTS, K, B), F32),
             pltpu.VMEM((N_GRP, SLOTS + 1, K, B), jnp.int16),
             pltpu.VMEM((K, B), F32),
             pltpu.VMEM((8, B), I32),
             pltpu.SMEM((8, B), I32),
+            pltpu.VMEM((R, K, 2 * B), BF16),
+            pltpu.VMEM((R, K, B), F32),
             dma((3,)),
             dma((6,)),
             dma((4,)),

time: 33.9 us -> 32.2 us (0.950)
  the two profiles are of different devices: /device:TPU:33 before, /device:TPU:0 now
where the time goes in v5:
time: 32.2 us; the launch traced here: 32.1 us
  Pallas kernels  31.4 us (98%)
  between operations  0.64 us (2%)
    pallas_call x1, Pallas kernels, on_device(): pl.pallas_call(product_kernel, in_specs=[hbm] * 4, out_specs=[vmem, any_]...  26.7 us
    pallas_call x1, Pallas kernels, on_device(): pl.pallas_call(coarse_kernel, in_specs=[vmem, any_], out_specs=[vmem, any...  4.7 us

profile of v5, /device:TPU:0, one launch (start us, length us, event | category | flops | bytes accessed | tf_op | source)
XLA Modules:
  0.0 32.1 jit_solution(2873833382510838475)
XLA Ops:
  0.6 26.7 %products.1 = (f32[64,16,128]{2,1,0:T(8,128)S(1)}, s16[16,9,16,128]{3,2,1,0:T(8,128)(2,1)S(1)}) custom-call(s32[8,64]{1,0:T(8,128)} %bitcast.2, s32[1,64]{1,0:T(1,128)} %bitcast.3, bf16[64,8,128,128]{3,2,1,0:T(8,128)(2,1)} %q_hbm.1, bf16[64,16,128]{2,1,0:T(8,128)(2,1)} %p_hbm.1), custom_call_target="tpu_custom_call" | custom-call | tf_op jit(solution)/shard_map/products/pallas_call | solution.py:327
  27.4 4.7 %coarse.1 = (f32[4,16,3072]{2,1,0:T(8,128)}, f32[64,16,128]{2,1,0:T(8,128)}) custom-call(s16[16,9,16,128]{3,2,1,0:T(8,128)(2,1)S(1)} %get-tuple-element.6.w, f32[64,16,128]{2,1,0:T(8,128)S(1)} %get-tuple-element.7.prod_in), custom_call_target="tpu_custom_call" | custom-call | tf_op jit(solution)/shard_map/coarse/pallas_call | solution.py:365

commit v6 on v5

--- a/solution.py
+++ b/solution.py
@@ -200,8 +200,8 @@
     order_copy.wait()
 
     def late(c):
-        for u in range(0, 16, 4):
-            ats = [c * 16 + u + d for d in range(4)]
+        for u in range(0, 8, 4):
+            ats = [c * 8 + u + d for d in range(4)]
             rows = [order_s[2, at] & (R - 1) for at in ats]
             for at, v in zip(ats, four_rows(rows, ats, LATE)):
                 prod_v[at] = v
@@ -244,16 +244,12 @@
 
     spot = iota((K, B), 1)
     late(0)
-    for c in range(1, R // 16):
-        two = (2 * c - 2, 2 * c - 1)
-        for s in two:
-            weights(s)
+    for c in range(1, R // 8):
+        weights(c - 1)
         late(c)
-        for s in two:
-            coded(s)
-        for s in two:
-            send(s)
-    begin = R // 8 - 2
+        coded(c - 1)
+        send(c - 1)
+    begin = R // 8 - 1
     weights(begin)
     for s in range(begin, N_GRP):
         if s + 1 < N_GRP:
@@ -304,13 +300,13 @@
 
     group = iota((K, B), 1) >> 4
 
-    @pl.loop(0, N_GRP // 4)
+    @pl.loop(0, N_GRP // 8)
     def _(j):
-        for u in range(4):
+        for u in range(8):
             for t in range(2):
                 for n in range(NB):
                     for a, acc in enumerate(accs):
-                        e = j * (4 * SLOTS) + (u * SLOTS + 2 * a + t)
+                        e = j * (8 * SLOTS) + (u * SLOTS + 2 * a + t)
                         one = jnp.where(group == n, rows[e], 0.0)
                         acc[chunk[n, e]] += pltpu.roll(one, turn[n, e], 1)
 

time: 32.2 us -> 31.9 us (level)
  no operation moved by 1% of the time
where the time goes in v6:
time: 31.9 us; the launch traced here: 31.8 us
  Pallas kernels  31.2 us (98%)
  between operations  0.64 us (2%)
    pallas_call x1, Pallas kernels, on_device(): pl.pallas_call(product_kernel, in_specs=[hbm] * 4, out_specs=[vmem, any_]...  26.6 us
    pallas_call x1, Pallas kernels, on_device(): pl.pallas_call(coarse_kernel, in_specs=[vmem, any_], out_specs=[vmem, any...  4.55 us

profile of v6, /device:TPU:0, one launch (start us, length us, event | category | flops | bytes accessed | tf_op | source)
XLA Modules:
  0.0 31.8 jit_solution(1876540754536852092)
XLA Ops:
  0.6 26.6 %products.1 = (f32[64,16,128]{2,1,0:T(8,128)S(1)}, s16[16,9,16,128]{3,2,1,0:T(8,128)(2,1)S(1)}) custom-call(s32[8,64]{1,0:T(8,128)} %bitcast.2, s32[1,64]{1,0:T(1,128)} %bitcast.3, bf16[64,8,128,128]{3,2,1,0:T(8,128)(2,1)} %q_hbm.1, bf16[64,16,128]{2,1,0:T(8,128)(2,1)} %p_hbm.1), custom_call_target="tpu_custom_call" | custom-call | tf_op jit(solution)/shard_map/products/pallas_call | solution.py:323
  27.3 4.6 %coarse.1 = (f32[4,16,3072]{2,1,0:T(8,128)}, f32[64,16,128]{2,1,0:T(8,128)}) custom-call(s16[16,9,16,128]{3,2,1,0:T(8,128)(2,1)S(1)} %get-tuple-element.6.w, f32[64,16,128]{2,1,0:T(8,128)S(1)} %get-tuple-element.7.prod_in), custom_call_target="tpu_custom_call" | custom-call | tf_op jit(solution)/shard_map/coarse/pallas_call | solution.py:361
